TPU v7x, 32 devices: a whole 2x2x4 slice. The times are simulated.
32 devices in a mesh: dp: 4 (over y, core), fsdp: 8 (over z, x).
Axes of the slice: x: 2, y: 2, z: 4, core: 2. Of those that a mesh axis runs over, the one named last changes fastest.
Arguments:
- frames: bfloat16 [16384, 768], P(('dp', 'fsdp')), may hold values from -6 to 6
- lengths: int32 [32, 2], P(('dp', 'fsdp')), may hold values from 0 to 512, as said below
- query_weight: bfloat16 [768, 768], P(('dp', 'fsdp')), may hold values from -0.21875 to 0.21875
- query_bias: bfloat16 [768], P(('dp', 'fsdp')), may hold values from -3 to 3
- key_weight: bfloat16 [768, 768], P(('dp', 'fsdp')), may hold values from -0.21875 to 0.21875
- value_weight: bfloat16 [768, 768], P(('dp', 'fsdp')), may hold values from -0.21875 to 0.21875
- value_bias: bfloat16 [768], P(('dp', 'fsdp')), may hold values from -3 to 3
- output_weight: bfloat16 [768, 768], P(('dp', 'fsdp')), may hold values from -2.5 to 2.5
- output_bias: bfloat16 [768], P(('dp', 'fsdp')), may hold values from -3 to 3
- first_gain: bfloat16 [768], P(('dp', 'fsdp')), may hold values from 0.5 to 1.5
- first_shift: bfloat16 [768], P(('dp', 'fsdp')), may hold values from -3 to 3
- inner_weight: bfloat16 [768, 3072], P(('dp', 'fsdp')), may hold values from -0.21875 to 0.21875
- inner_bias: bfloat16 [3072], P(('dp', 'fsdp')), may hold values from -3 to 3
- outer_weight: bfloat16 [3072, 768], P(('dp', 'fsdp')), may hold values from -0.109375 to 0.109375
- outer_bias: bfloat16 [768], P(('dp', 'fsdp')), may hold values from -3 to 3
- second_gain: bfloat16 [768], P(('dp', 'fsdp')), may hold values from 0.5 to 1.5
- second_shift: bfloat16 [768], P(('dp', 'fsdp')), may hold values from -3 to 3
- grad_out: bfloat16 [16384, 768], P(('dp', 'fsdp')), may hold values from -6 to 6
Outputs:
- layer_out: bfloat16 [16384, 768], P(('dp', 'fsdp'))
- frames_grad: bfloat16 [16384, 768], P(('dp', 'fsdp'))
- query_weight_grad: float32 [768, 768], P(('dp', 'fsdp'))
- query_bias_grad: float32 [768], P(('dp', 'fsdp'))
- key_weight_grad: float32 [768, 768], P(('dp', 'fsdp'))
- value_weight_grad: float32 [768, 768], P(('dp', 'fsdp'))
- value_bias_grad: float32 [768], P(('dp', 'fsdp'))
- output_weight_grad: float32 [768, 768], P(('dp', 'fsdp'))
- output_bias_grad: float32 [768], P(('dp', 'fsdp'))
- first_gain_grad: float32 [768], P(('dp', 'fsdp'))
- first_shift_grad: float32 [768], P(('dp', 'fsdp'))
- inner_weight_grad: float32 [768, 3072], P(('dp', 'fsdp'))
- inner_bias_grad: float32 [3072], P(('dp', 'fsdp'))
- outer_weight_grad: float32 [3072, 768], P(('dp', 'fsdp'))
- outer_bias_grad: float32 [768], P(('dp', 'fsdp'))
- second_gain_grad: float32 [768], P(('dp', 'fsdp'))
- second_shift_grad: float32 [768], P(('dp', 'fsdp'))
Inputs may be any that keep to these rules, and one draw needn't show every extreme that they name: `lengths`: row b holds block b's two utterances: slot 0 has 100 to 512 frames, slot 1 has 0 (empty) up to 512 minus slot 0; the block's remaining slots are padding. In one block, drawn from the seed, slot 0 fills all 512 slots.
All inputs are finite; a program needn't handle non-finite values.
Results may differ from a plain program's by a relative error of at most 0.015.
Values may be sent and summed in bfloat16 or wider, within the bound.
A program may use at most 192 MiB of HBM per device.

v0:
```python
import jax
import jax.numpy as jnp
from jax import lax
from jax.sharding import PartitionSpec as P

HEADS = 12


def layer_norm(values, gain_vec, shift_vec):
    center = values - jnp.mean(values, axis=-1, keepdims=True)
    spread = jnp.mean(center * center, axis=-1, keepdims=True)
    return center * lax.rsqrt(spread + 1e-05) * gain_vec + shift_vec


def exact_gelu(values):
    return jax.nn.gelu(values, approximate=False)


def matmul(left_side, right_side):
    return jnp.dot(left_side, right_side, preferred_element_type=jnp.float32)


def matmul_tn(left_side, right_side):
    return lax.dot_general(
        left_side, right_side, (((0,), (0,)), ((), ())), preferred_element_type=jnp.float32
    )


def matmul_nt(left_side, right_side):
    return lax.dot_general(
        left_side, right_side, (((1,), (1,)), ((), ())), preferred_element_type=jnp.float32
    )


def column_sums(values):
    return jnp.sum(values.astype(jnp.float32), axis=0)


def block_scores(query_block, key_heads, group_block, groups, score_scale):
    raw_scores = (
        jnp.einsum("qhd,khd->hqk", query_block, key_heads, preferred_element_type=jnp.float32)
        * score_scale
    )
    allowed = group_block[:, None] == groups[None, :]
    return jnp.where(allowed[None], raw_scores, -1e30)


def per_device(
    frames,
    lengths,
    query_weight,
    query_bias,
    key_weight,
    value_weight,
    value_bias,
    output_weight,
    output_bias,
    first_gain,
    first_shift,
    inner_weight,
    inner_bias,
    outer_weight,
    outer_bias,
    second_gain,
    second_shift,
    grad_out,
):
    frame_count = frames.shape[0]
    model_width = frames.shape[1]
    head_size = model_width // HEADS
    score_scale = head_size ** (-0.5)
    places = jnp.arange(frame_count, dtype=jnp.int32)
    bounds = jnp.cumsum(lengths[0])
    groups = jnp.sum((places[:, None] >= bounds[None, :]).astype(jnp.int32), axis=1)
    live_mask = (places < bounds[-1]).astype(jnp.float32)
    gathered = (
        lax.all_gather(query_weight, ("dp", "fsdp"), axis=0, tiled=True),
        lax.all_gather(query_bias, ("dp", "fsdp"), axis=0, tiled=True),
        lax.all_gather(key_weight, ("dp", "fsdp"), axis=0, tiled=True),
        lax.all_gather(value_weight, ("dp", "fsdp"), axis=0, tiled=True),
        lax.all_gather(value_bias, ("dp", "fsdp"), axis=0, tiled=True),
        lax.all_gather(output_weight, ("dp", "fsdp"), axis=0, tiled=True),
        lax.all_gather(output_bias, ("dp", "fsdp"), axis=0, tiled=True),
        lax.all_gather(first_gain, ("dp", "fsdp"), axis=0, tiled=True),
        lax.all_gather(first_shift, ("dp", "fsdp"), axis=0, tiled=True),
        lax.all_gather(inner_weight, ("dp", "fsdp"), axis=0, tiled=True),
        lax.all_gather(inner_bias, ("dp", "fsdp"), axis=0, tiled=True),
        lax.all_gather(outer_weight, ("dp", "fsdp"), axis=0, tiled=True),
        lax.all_gather(outer_bias, ("dp", "fsdp"), axis=0, tiled=True),
        lax.all_gather(second_gain, ("dp", "fsdp"), axis=0, tiled=True),
        lax.all_gather(second_shift, ("dp", "fsdp"), axis=0, tiled=True),
    )
    (
        query_mat,
        query_vec,
        key_mat,
        value_mat,
        value_vec,
        output_mat,
        output_vec,
        first_scale,
        first_offset,
        inner_mat,
        inner_vec,
        outer_mat,
        outer_vec,
        second_scale,
        second_offset,
    ) = gathered
    query_rows = (matmul(frames, query_mat) + query_vec.astype(jnp.float32)).astype(jnp.bfloat16)
    key_rows = matmul(frames, key_mat).astype(jnp.bfloat16)
    value_rows = (matmul(frames, value_mat) + value_vec.astype(jnp.float32)).astype(jnp.bfloat16)
    query_heads = query_rows.reshape(frame_count, HEADS, head_size)
    key_heads = key_rows.reshape(frame_count, HEADS, head_size)
    value_heads = value_rows.reshape(frame_count, HEADS, head_size)
    scores = block_scores(query_heads, key_heads, groups, groups, score_scale)
    row_max = jnp.max(scores, axis=-1, keepdims=True)
    raw_weights = jnp.exp(scores - row_max)
    row_total = jnp.sum(raw_weights, axis=-1, keepdims=True)
    attn_prob = raw_weights / row_total
    log_totals = row_max + jnp.log(row_total)
    context_parts = jnp.einsum(
        "hqk,khd->qhd",
        attn_prob.astype(jnp.bfloat16),
        value_heads,
        preferred_element_type=jnp.float32,
    )
    context_rows = context_parts.reshape(frame_count, model_width).astype(jnp.bfloat16)
    frames_float = frames.astype(jnp.float32)
    resid_one = frames_float + matmul(context_rows, output_mat) + output_vec.astype(jnp.float32)
    hidden, first_pull = jax.vjp(
        layer_norm, resid_one, first_scale.astype(jnp.float32), first_offset.astype(jnp.float32)
    )
    hidden_low = hidden.astype(jnp.bfloat16)
    inner_pre = matmul(hidden_low, inner_mat) + inner_vec.astype(jnp.float32)
    active, gelu_pull = jax.vjp(exact_gelu, inner_pre)
    active_low = active.astype(jnp.bfloat16)
    outer_out = matmul(active_low, outer_mat) + outer_vec.astype(jnp.float32)
    normed_out, second_pull = jax.vjp(
        layer_norm,
        hidden + outer_out,
        second_scale.astype(jnp.float32),
        second_offset.astype(jnp.float32),
    )
    layer_out = (normed_out * live_mask[:, None]).astype(jnp.bfloat16)
    regathered = (
        lax.all_gather(query_weight, ("dp", "fsdp"), axis=0, tiled=True),
        lax.all_gather(key_weight, ("dp", "fsdp"), axis=0, tiled=True),
        lax.all_gather(value_weight, ("dp", "fsdp"), axis=0, tiled=True),
        lax.all_gather(output_weight, ("dp", "fsdp"), axis=0, tiled=True),
        lax.all_gather(inner_weight, ("dp", "fsdp"), axis=0, tiled=True),
        lax.all_gather(outer_weight, ("dp", "fsdp"), axis=0, tiled=True),
    )
    query_mat, key_mat, value_mat, output_mat, inner_mat, outer_mat = regathered
    grad_top = grad_out.astype(jnp.float32) * live_mask[:, None]
    grad_two, second_gain_grad, second_shift_grad = second_pull(grad_top)
    grad_outer = grad_two.astype(jnp.bfloat16)
    outer_mat_grad = matmul_tn(active_low, grad_outer)
    outer_vec_grad = column_sums(grad_outer)
    (grad_inner,) = gelu_pull(matmul_nt(grad_outer, outer_mat))
    grad_inner_low = grad_inner.astype(jnp.bfloat16)
    inner_mat_grad = matmul_tn(hidden_low, grad_inner_low)
    inner_vec_grad = column_sums(grad_inner_low)
    grad_hidden = grad_two + matmul_nt(grad_inner_low, inner_mat)
    grad_one, first_gain_grad, first_shift_grad = first_pull(grad_hidden)
    grad_attn = grad_one.astype(jnp.bfloat16)
    output_mat_grad = matmul_tn(context_rows, grad_attn)
    output_vec_grad = column_sums(grad_attn)
    grad_context = (
        matmul_nt(grad_attn, output_mat).astype(jnp.bfloat16).reshape(frame_count, HEADS, head_size)
    )
    scores = block_scores(query_heads, key_heads, groups, groups, score_scale)
    attn_prob = jnp.exp(scores - log_totals)
    grad_prob = jnp.einsum(
        "qhd,khd->hqk", grad_context, value_heads, preferred_element_type=jnp.float32
    )
    inner_sum = jnp.sum(attn_prob * grad_prob, axis=-1, keepdims=True)
    grad_scores = (attn_prob * (grad_prob - inner_sum)).astype(jnp.bfloat16)
    query_grad_parts = (
        jnp.einsum("hqk,khd->qhd", grad_scores, key_heads, preferred_element_type=jnp.float32)
        * score_scale
    )
    key_grad_sum = (
        jnp.einsum("hqk,qhd->khd", grad_scores, query_heads, preferred_element_type=jnp.float32)
        * score_scale
    )
    value_grad_sum = jnp.einsum(
        "hqk,qhd->khd",
        attn_prob.astype(jnp.bfloat16),
        grad_context,
        preferred_element_type=jnp.float32,
    )
    grad_query = query_grad_parts.reshape(frame_count, model_width).astype(jnp.bfloat16)
    grad_key = key_grad_sum.reshape(frame_count, model_width).astype(jnp.bfloat16)
    grad_value = value_grad_sum.reshape(frame_count, model_width).astype(jnp.bfloat16)
    query_mat_grad = matmul_tn(frames, grad_query)
    query_vec_grad = column_sums(grad_query)
    key_mat_grad = matmul_tn(frames, grad_key)
    value_mat_grad = matmul_tn(frames, grad_value)
    value_vec_grad = column_sums(grad_value)
    frames_grad = (
        grad_one
        + matmul_nt(grad_query, query_mat)
        + matmul_nt(grad_key, key_mat)
        + matmul_nt(grad_value, value_mat)
    ).astype(jnp.bfloat16)
    shares = (
        lax.psum_scatter(query_mat_grad, ("dp", "fsdp"), scatter_dimension=0, tiled=True),
        lax.psum_scatter(query_vec_grad, ("dp", "fsdp"), scatter_dimension=0, tiled=True),
        lax.psum_scatter(key_mat_grad, ("dp", "fsdp"), scatter_dimension=0, tiled=True),
        lax.psum_scatter(value_mat_grad, ("dp", "fsdp"), scatter_dimension=0, tiled=True),
        lax.psum_scatter(value_vec_grad, ("dp", "fsdp"), scatter_dimension=0, tiled=True),
        lax.psum_scatter(output_mat_grad, ("dp", "fsdp"), scatter_dimension=0, tiled=True),
        lax.psum_scatter(output_vec_grad, ("dp", "fsdp"), scatter_dimension=0, tiled=True),
        lax.psum_scatter(first_gain_grad, ("dp", "fsdp"), scatter_dimension=0, tiled=True),
        lax.psum_scatter(first_shift_grad, ("dp", "fsdp"), scatter_dimension=0, tiled=True),
        lax.psum_scatter(inner_mat_grad, ("dp", "fsdp"), scatter_dimension=0, tiled=True),
        lax.psum_scatter(inner_vec_grad, ("dp", "fsdp"), scatter_dimension=0, tiled=True),
        lax.psum_scatter(outer_mat_grad, ("dp", "fsdp"), scatter_dimension=0, tiled=True),
        lax.psum_scatter(outer_vec_grad, ("dp", "fsdp"), scatter_dimension=0, tiled=True),
        lax.psum_scatter(second_gain_grad, ("dp", "fsdp"), scatter_dimension=0, tiled=True),
        lax.psum_scatter(second_shift_grad, ("dp", "fsdp"), scatter_dimension=0, tiled=True),
    )
    return (
        layer_out,
        frames_grad,
        shares[0],
        shares[1],
        shares[2],
        shares[3],
        shares[4],
        shares[5],
        shares[6],
        shares[7],
        shares[8],
        shares[9],
        shares[10],
        shares[11],
        shares[12],
        shares[13],
        shares[14],
    )


def solution(mesh):
    in_specs = (
        P(("dp", "fsdp"), None),
        P(("dp", "fsdp"), None),
        P(("dp", "fsdp"), None),
        P(("dp", "fsdp")),
        P(("dp", "fsdp"), None),
        P(("dp", "fsdp"), None),
        P(("dp", "fsdp")),
        P(("dp", "fsdp"), None),
        P(("dp", "fsdp")),
        P(("dp", "fsdp")),
        P(("dp", "fsdp")),
        P(("dp", "fsdp"), None),
        P(("dp", "fsdp")),
        P(("dp", "fsdp"), None),
        P(("dp", "fsdp")),
        P(("dp", "fsdp")),
        P(("dp", "fsdp")),
        P(("dp", "fsdp"), None),
    )
    out_specs = (
        P(("dp", "fsdp"), None),
        P(("dp", "fsdp"), None),
        P(("dp", "fsdp"), None),
        P(("dp", "fsdp")),
        P(("dp", "fsdp"), None),
        P(("dp", "fsdp"), None),
        P(("dp", "fsdp")),
        P(("dp", "fsdp"), None),
        P(("dp", "fsdp")),
        P(("dp", "fsdp")),
        P(("dp", "fsdp")),
        P(("dp", "fsdp"), None),
        P(("dp", "fsdp")),
        P(("dp", "fsdp"), None),
        P(("dp", "fsdp")),
        P(("dp", "fsdp")),
        P(("dp", "fsdp")),
    )
    return jax.shard_map(
        per_device, mesh=mesh, in_specs=in_specs, out_specs=out_specs, check_vma=False
    )
```

profile of v0, /device:TPU:0, one launch (start us, length us, event | category | flops | bytes accessed | tf_op | source)
XLA Modules:
  0.0 1126.2 jit_solution(8192119810610155402)
XLA Ops:
  18.8 42.6 %all-reduce.19 = (bf16[768]{0:T(1024)(128)(2,1)S(1)}, bf16[768]{0:T(1024)(128)(2,1)S(1)}, bf16[768]{0:T(1024)(128)(2,1)S(1)}, bf16[768]{0:T(1024)(128)(2,1)S(1)}...) all-reduce(bf16[768]{0:T(1024)(128)(2,1)S(1)} %dynamic-update-slice, ...), channel_id=1, replica_groups=mesh['dp'=4,'fsdp'=8] {'dp','fsdp'}, use_global_device_ids=true, to_apply=%add | all-reduce | flops 9216 | bytes 36864
  63.8 4.3 all-gather.7.cloned.1.call-done
  70.4 54.0 %all-gather.9.cloned.1.call-done = bf16[768,768]{1,0:T(8,128)(2,1)} async-done(((bf16[24,768]{1,0:T(8,128)(2,1)}), bf16[768,768]{1,0:T(8,128)(2,1)}) %all-gather.9.cloned.1.call-update) | async-done | bytes 1179664 | tf_op jit(solution)/shard_map/all_gather | solution.py:77
  124.4 2.9 add_convert_fusion.2
  129.3 51.2 %all-gather.11.cloned.1.call-done = bf16[768,768]{1,0:T(8,128)(2,1)} async-done(((bf16[24,768]{1,0:T(8,128)(2,1)}), bf16[768,768]{1,0:T(8,128)(2,1)}) %all-gather.11.cloned.1.call-update) | async-done | bytes 1179664 | tf_op jit(solution)/shard_map/all_gather | solution.py:79
  180.5 2.9 convolution_convert_fusion.1
  186.9 2.6 fusion
  191.5 4.4 fusion.18
  195.8 40.6 %all-gather.13.cloned.1.call-done = bf16[768,768]{1,0:T(8,128)(2,1)} async-done(((bf16[24,768]{1,0:T(8,128)(2,1)}), bf16[768,768]{1,0:T(8,128)(2,1)}) %all-gather.13.cloned.1.call-update) | async-done | bytes 1179664 | tf_op jit(solution)/shard_map/all_gather | solution.py:82
  236.5 2.4 fusion.35
  240.4 61.6 %all-gather.15.cloned.1.call-done = bf16[768,3072]{1,0:T(8,128)(2,1)} async-done(((bf16[24,3072]{1,0:T(8,128)(2,1)}), bf16[768,3072]{1,0:T(8,128)(2,1)}) %all-gather.15.cloned.1.call-update) | async-done | bytes 4718608 | tf_op jit(solution)/shard_map/all_gather | solution.py:86
  301.9 21.0 %multiply_convert_fusion.1 = (bf16[512,3072]{1,0:T(8,128)(2,1)}, f32[512,3072]{1,0:T(8,128)}, f32[512,3072]{1,0:T(8,128)}) fusion(f32[3072]{0:T(1024)S(1)} %convert_element_type.159, bf16[768,3072]{1,0:T(8,128)(2,1)} %all-gather.15.cloned.1.call-done, f32[512,768]{1,0:T(8,128)} %copy-done.7, f32[768]{0:T(1024)S(1)} %convert_element_type.157, ...), kind=kOutput, calls=%fused_computation.14 | convolution fusion | flops 2521694208 | bytes 22042624 | tf_op jit(solution)/shard_map/dot_general | solution.py:20
  322.9 44.4 %all-gather.17.cloned.1.call-done = bf16[3072,768]{1,0:T(8,128)(2,1)} async-done(((bf16[96,768]{1,0:T(8,128)(2,1)}), bf16[3072,768]{1,0:T(8,128)(2,1)}) %all-gather.17.cloned.1.call-update) | async-done | bytes 4718608 | tf_op jit(solution)/shard_map/all_gather | solution.py:88
  367.3 6.1 fusion.36
  377.2 8.5 convert_reduce_fusion
  385.7 3.1 multiply_reduce_fusion.2
  394.7 13.5 %multiply_reduce_fusion = (f32[12,512]{1,0:T(8,128)S(1)}, f32[12,512,512]{1,2,0:T(8,128)}) fusion(f32[12,512]{1,0:T(8,128)S(1)} %log_add_fusion, f32[12,512,512]{1,2,0:T(8,128)} %copy-done, pred[512,512]{0,1:T(8,128)(4,1)S(1)} %broadcast_compare_fusion, bf16[512,12,64]{0,2,1:T(8,128)(2,1)} %bitcast.82, bf16[512,12,64]{0,2,1:T(8,128)(2,1)} %bitcast.81), kind=kOutput, calls=%fused_computation.1 | convolution fusion | flops 418375680 | bytes 27049984 | tf_op jit(solution)/shard_map/qhd,khd->hqk/dot_general | solution.py:174
  408.3 7.0 multiply_convert_fusion
  421.0 3.1 copy.87
  424.4 4.8 multiply_convert_fusion.2
  432.3 3.2 copy.89
  435.6 6.6 convert_reduce_fusion.3
  445.3 3.2 copy.91
  448.6 3.7 fusion.39
  452.4 7.2 fusion.28
  460.8 8.2 fusion.40
  469.2 40.8 %all-reduce.18 = (f32[768]{0:T(1024)S(1)}, f32[768]{0:T(1024)S(1)}, f32[768]{0:T(1024)S(1)}, f32[768]{0:T(1024)S(1)}, f32[768]{0:T(1024)S(1)}, /*index=5*/f32[30...) all-reduce(f32[768]{0:T(1024)S(1)} %reduce_sum.228, ...), channel_id=3, replica_groups=mesh['dp'=4,'fsdp'=8] {'dp','fsdp'}, use_global_device_ids=true, to_apply=%region_15.16.clone | all-reduce | flops 9216 | bytes 73728
  522.3 104.8 %reduce-scatter.21.cloned.1.call-done = f32[24,768]{1,0:T(8,128)} async-done(((f32[768,768]{1,0:T(8,128)}), f32[24,768]{1,0:T(8,128)}) %reduce-scatter.21.cloned.1.call-update) | async-done | bytes 73744
  627.1 103.9 %reduce-scatter.23.cloned.1.call-done = f32[24,768]{1,0:T(8,128)} async-done(((f32[768,768]{1,0:T(8,128)}), f32[24,768]{1,0:T(8,128)}) %reduce-scatter.23.cloned.1.call-update) | async-done | bytes 73744
  731.0 104.7 %reduce-scatter.13.cloned.1.call-done = f32[24,768]{1,0:T(8,128)} async-done(((f32[768,768]{1,0:T(8,128)}), f32[24,768]{1,0:T(8,128)}) %reduce-scatter.13.cloned.1.call-update) | async-done | bytes 73744 | tf_op jit(solution)/shard_map/reduce_scatter | solution.py:213
  835.7 141.2 %reduce-scatter.15.cloned.1.call-done = f32[24,3072]{1,0:T(8,128)} async-done(((f32[768,3072]{1,0:T(8,128)}), f32[24,3072]{1,0:T(8,128)}) %reduce-scatter.15.cloned.1.call-update) | async-done | bytes 294928 | tf_op jit(solution)/shard_map/reduce_scatter | solution.py:217
  976.8 142.0 %reduce-scatter.17.cloned.1.call-done = f32[96,768]{1,0:T(8,128)} async-done(((f32[3072,768]{1,0:T(8,128)}), f32[96,768]{1,0:T(8,128)}) %reduce-scatter.17.cloned.1.call-update) | async-done | bytes 294928 | tf_op jit(solution)/shard_map/reduce_scatter | solution.py:219
  (162 shorter events, 60.5 us)
Async XLA Ops:
  7.2 117.2 %copy-start.2 = (bf16[512,768]{1,0:T(8,128)(2,1)S(1)}, bf16[512,768]{1,0:T(8,128)(2,1)}, u32[]{:S(2)}) copy-start(bf16[512,768]{1,0:T(8,128)(2,1)} %param.18) | copy-start | bytes 2359300
  7.2 60.9 %all-gather.7.cloned.1.call-start = ((), (), s32[]{:S(2)}) async-start(), calls=%async_computation.6 | async-start | bytes 1216512 | tf_op jit(solution)/shard_map/all_gather | solution.py:80
  7.9 116.4 %all-gather.9.cloned.1.call-start = ((), (), s32[]{:S(2)}) async-start(), calls=%async_computation.7 | async-start | bytes 1216512 | tf_op jit(solution)/shard_map/all_gather | solution.py:77
  8.7 171.8 %all-gather.11.cloned.1.call-start = ((), (), s32[]{:S(2)}) async-start(), calls=%async_computation.8 | async-start | bytes 1216512 | tf_op jit(solution)/shard_map/all_gather | solution.py:79
  9.4 227.0 %all-gather.13.cloned.1.call-start = ((), (), s32[]{:S(2)}) async-start(), calls=%async_computation.9 | async-start | bytes 1216512 | tf_op jit(solution)/shard_map/all_gather | solution.py:82
  10.0 292.0 %all-gather.15.cloned.1.call-start = ((), (), s32[]{:S(2)}) async-start(), calls=%async_computation.10 | async-start | bytes 4866048 | tf_op jit(solution)/shard_map/all_gather | solution.py:86
  10.6 356.7 %all-gather.17.cloned.1.call-start = ((), (), s32[]{:S(2)}) async-start(), calls=%async_computation.11 | async-start | bytes 4866048 | tf_op jit(solution)/shard_map/all_gather | solution.py:88
  11.2 511.1 %reduce-scatter.19.cloned.1.call-start = ((), (), s32[]{:S(2)}) async-start(), calls=%async_computation.15 | async-start | bytes 2433024
  127.6 61.9 %copy-start.11 = (bf16[512,768]{0,1:T(8,128)(2,1)}, bf16[512,768]{0,1:T(8,128)(2,1)S(1)}, u32[]{:S(2)}) copy-start(bf16[512,768]{0,1:T(8,128)(2,1)S(1)} %copy.72) | copy-start | bytes 2359300
  186.9 4.6 copy-start
  240.4 126.9 %copy-start.8 = (f32[512,768]{1,0:T(8,128)S(1)}, f32[512,768]{1,0:T(8,128)}, u32[]{:S(2)}) copy-start(f32[512,768]{1,0:T(8,128)} %copy-done.7) | copy-start | bytes 4718596
  367.3 6.4 copy-start.13
  376.3 9.4 slice-start.3
  376.5 9.2 copy-start.20
  377.2 8.5 slice-start.4
  385.7 3.2 copy-start.25
  385.7 3.2 copy-start.9
  394.7 13.5 %slice-start = ((s8[12582912]{0:T(1024)(128)(4,1)}), s8[4194304]{0:T(1024)(128)(4,1)S(1)}, s32[]{:S(2)}) async-start(s8[12582912]{0:T(1024)(128)(4,1)} %bitcast.72), calls=%async_computation.18 | async-start | bytes 8388608
  394.7 13.5 %slice-start.1 = ((s8[12582912]{0:T(1024)(128)(4,1)}), s8[4194304]{0:T(1024)(128)(4,1)S(1)}, s32[]{:S(2)}) async-start(s8[12582912]{0:T(1024)(128)(4,1)} %bitcast.72), calls=%async_computation.19 | async-start | bytes 8388608
  394.7 13.5 %slice-start.2 = ((s8[12582912]{0:T(1024)(128)(4,1)}), s8[4194304]{0:T(1024)(128)(4,1)S(1)}, s32[]{:S(2)}) async-start(s8[12582912]{0:T(1024)(128)(4,1)} %bitcast.72), calls=%async_computation.20 | async-start | bytes 8388608
  415.3 3.5 copy-start.3
  424.1 6.0 copy-start.4
  424.1 203.0 %reduce-scatter.21.cloned.1.call-start = ((), (), s32[]{:S(2)}) async-start(), calls=%async_computation.16 | async-start | bytes 2433024
  432.3 3.3 copy-start.12
  435.5 295.5 %reduce-scatter.23.cloned.1.call-start = ((), (), s32[]{:S(2)}) async-start(), calls=%async_computation.17 | async-start | bytes 2433024
  448.5 3.8 copy-start.10
  448.5 387.1 %reduce-scatter.13.cloned.1.call-start = ((), (), s32[]{:S(2)}) async-start(), calls=%async_computation.12 | async-start | bytes 2433024 | tf_op jit(solution)/shard_map/reduce_scatter | solution.py:213
  452.3 524.5 %reduce-scatter.15.cloned.1.call-start = ((), (), s32[]{:S(2)}) async-start(), calls=%async_computation.13 | async-start | bytes 9732096 | tf_op jit(solution)/shard_map/reduce_scatter | solution.py:217
  459.6 659.2 %reduce-scatter.17.cloned.1.call-start = ((), (), s32[]{:S(2)}) async-start(), calls=%async_computation.14 | async-start | bytes 9732096 | tf_op jit(solution)/shard_map/reduce_scatter | solution.py:219
  469.0 46.3 %copy-start.18 = (bf16[12,64,512]{2,1,0:T(8,128)(2,1)S(1)}, bf16[12,64,512]{2,1,0:T(8,128)(2,1)}, u32[]{:S(2)}) copy-start(bf16[12,64,512]{2,1,0:T(8,128)(2,1)} %copy-done.17) | copy-start | bytes 2359300
  469.0 48.5 %copy-start.6 = (bf16[12,64,512]{2,1,0:T(8,128)(2,1)S(1)}, bf16[12,64,512]{2,1,0:T(8,128)(2,1)}, u32[]{:S(2)}) copy-start(bf16[12,64,512]{2,1,0:T(8,128)(2,1)} %copy-done.5) | copy-start | bytes 2359300
  510.0 7.5 copy-start.23
  (11 other events, 19.1 us)
Sparse Core Ops, SparseCore 0:
  11.0 57.0 all-gather.6
  71.1 53.2 all-gather.8
  127.4 53.0 all-gather.10
  183.3 53.0 all-gather.12
  239.3 62.6 all-gather.14
  304.8 62.4 all-gather.16
  424.2 98.0 reduce-scatter.18
  529.0 98.0 reduce-scatter.20
  632.9 98.0 reduce-scatter.22
  737.6 98.0 reduce-scatter.12
  842.1 134.6 reduce-scatter.14
  984.2 134.6 reduce-scatter.16
where the time goes:
time: 1140 us; the launch traced here: 1130 us
  waiting for transfers between devices  858 us (75%)
  matrix products  114 us (10%)
  blocking collectives  83.4 us (7%)
  local copies, waits for them, and re-layouts  38.6 us (3%)
  other arithmetic  15.6 us (1%)
  between operations  15.2 us (1%)
    unnamed x15, waiting for transfers between devices  214 us
    reduce_scatter x1, waiting for transfers between devices, per_device(): lax.psum_scatter(outer_mat_grad, ('dp', 'fsdp'), scatter_dimension=0, til...  142 us
    reduce_scatter x1, waiting for transfers between devices, per_device(): lax.psum_scatter(inner_mat_grad, ('dp', 'fsdp'), scatter_dimension=0, til...  141 us
    reduce_scatter x1, waiting for transfers between devices, per_device(): lax.psum_scatter(output_mat_grad, ('dp', 'fsdp'), scatter_dimension=0, ti...  105 us
    unnamed x2, blocking collectives  83.4 us
    all_gather x1, waiting for transfers between devices, per_device(): lax.all_gather(inner_weight, ('dp', 'fsdp'), axis=0, tiled=True)  61.6 us
    all_gather x1, waiting for transfers between devices, per_device(): lax.all_gather(query_weight, ('dp', 'fsdp'), axis=0, tiled=True)  54 us
    all_gather x1, waiting for transfers between devices, per_device(): lax.all_gather(key_weight, ('dp', 'fsdp'), axis=0, tiled=True)  51.2 us
  transfers between devices with their start and end apart: 12, of which 12 were waited for; matrix products, arithmetic and copies ran while one was open for 9% of the time, Pallas kernels for 0%

commit v1 on v0

--- a/solution.py
+++ b/solution.py
@@ -4,6 +4,18 @@
 from jax.sharding import PartitionSpec as P
 
 HEADS = 12
+
+
+def doubled_up(x, axis, dim):
+    ways, here = (lax.axis_size(axis), lax.axis_index(axis))
+    grown, reach = (x, 1)
+    while reach < ways:
+        theirs = lax.ppermute(grown, axis, [(d, d ^ reach) for d in range(ways)])
+        mine_first = jnp.concatenate([grown, theirs], axis=dim)
+        theirs_first = jnp.concatenate([theirs, grown], axis=dim)
+        grown = jnp.where(here & reach == 0, mine_first, theirs_first)
+        reach = 2 * reach
+    return grown
 
 
 def layer_norm(values, gain_vec, shift_vec):
@@ -79,7 +91,7 @@
         lax.all_gather(key_weight, ("dp", "fsdp"), axis=0, tiled=True),
         lax.all_gather(value_weight, ("dp", "fsdp"), axis=0, tiled=True),
         lax.all_gather(value_bias, ("dp", "fsdp"), axis=0, tiled=True),
-        lax.all_gather(output_weight, ("dp", "fsdp"), axis=0, tiled=True),
+        doubled_up(output_weight, ("dp", "fsdp"), 0),
         lax.all_gather(output_bias, ("dp", "fsdp"), axis=0, tiled=True),
         lax.all_gather(first_gain, ("dp", "fsdp"), axis=0, tiled=True),
         lax.all_gather(first_shift, ("dp", "fsdp"), axis=0, tiled=True),

time: 1140 us -> 1110 us (0.974)
  waiting for transfers between devices: 858 us -> 827 us
    all_gather x1, waiting for transfers between devices: 61.6 us -> 46.7 us  [per_device(): lax.all_gather(inner_weight, ('dp', 'fsdp'), axis=0, tiled=True)]
    all_gather x1, waiting for transfers between devices: 54 us -> 42 us  [per_device(): lax.all_gather(query_weight, ('dp', 'fsdp'), axis=0, tiled=True)]
    unnamed x92 -> x90, local copies, waits for them, and re-layouts: 32.1 us -> 31.2 us
  transfers between devices with their start and end apart: 12 -> 17, of which waited for: 12 -> 14; matrix products, arithmetic and copies ran while one was open for 9% -> 12% of each run, Pallas kernels for 0% -> 0%
where the time goes in v1:
time: 1110 us; the launch traced here: 1100 us
  waiting for transfers between devices  827 us (75%)
  matrix products  115 us (10%)
  blocking collectives  81.8 us (7%)
  local copies, waits for them, and re-layouts  36.2 us (3%)
  other arithmetic  18.4 us (2%)
  between operations  15.2 us (1%)
  starting transfers between devices  11.4 us (1%)
    unnamed x15, waiting for transfers between devices  215 us
    reduce_scatter x1, waiting for transfers between devices, per_device(): lax.psum_scatter(outer_mat_grad, ('dp', 'fsdp'), scatter_dimension=0, til...  142 us
    reduce_scatter x1, waiting for transfers between devices, per_device(): lax.psum_scatter(inner_mat_grad, ('dp', 'fsdp'), scatter_dimension=0, til...  141 us
    reduce_scatter x1, waiting for transfers between devices, per_device(): lax.psum_scatter(output_mat_grad, ('dp', 'fsdp'), scatter_dimension=0, ti...  105 us
    unnamed x2, blocking collectives  81.8 us
    all_gather x1, waiting for transfers between devices, per_device(): lax.all_gather(key_weight, ('dp', 'fsdp'), axis=0, tiled=True)  53.8 us
    all_gather x1, waiting for transfers between devices, per_device(): lax.all_gather(inner_weight, ('dp', 'fsdp'), axis=0, tiled=True)  46.7 us
    all_gather x1, waiting for transfers between devices, per_device(): lax.all_gather(outer_weight, ('dp', 'fsdp'), axis=0, tiled=True)  44.4 us
  transfers between devices with their start and end apart: 17, of which 14 were waited for; matrix products, arithmetic and copies ran while one was open for 12% of the time, Pallas kernels for 0%

profile of v1, /device:TPU:0, one launch (start us, length us, event | category | flops | bytes accessed | tf_op | source)
XLA Modules:
  0.0 1104.5 jit_solution(8416821745512684951)
XLA Ops:
  10.6 3.0 collective-permute-start
  21.2 3.1 collective-permute-start.2
  31.9 41.2 %all-reduce.19 = (bf16[768]{0:T(1024)(128)(2,1)S(1)}, bf16[768]{0:T(1024)(128)(2,1)S(1)}, bf16[768]{0:T(1024)(128)(2,1)S(1)}, bf16[768]{0:T(1024)(128)(2,1)S(1)}...) all-reduce(bf16[768]{0:T(1024)(128)(2,1)S(1)} %dynamic-update-slice, ...), channel_id=1, replica_groups=mesh['dp'=4,'fsdp'=8] {'dp','fsdp'}, use_global_device_ids=true, to_apply=%add | all-reduce | flops 9216 | bytes 36864
  82.3 42.0 %all-gather.9.cloned.1.call-done = bf16[768,768]{1,0:T(8,128)(2,1)} async-done(((bf16[24,768]{1,0:T(8,128)(2,1)}), bf16[768,768]{1,0:T(8,128)(2,1)}) %all-gather.9.cloned.1.call-update) | async-done | bytes 1179664 | tf_op jit(solution)/shard_map/all_gather | solution.py:89
  126.6 53.8 %all-gather.11.cloned.1.call-done = bf16[768,768]{1,0:T(8,128)(2,1)} async-done(((bf16[24,768]{1,0:T(8,128)(2,1)}), bf16[768,768]{1,0:T(8,128)(2,1)}) %all-gather.11.cloned.1.call-update) | async-done | bytes 1179664 | tf_op jit(solution)/shard_map/all_gather | solution.py:91
  180.4 2.9 convolution_convert_fusion.1
  191.4 3.6 fusion.18
  195.0 2.8 fusion.42
  199.3 46.7 %all-gather.13.cloned.1.call-done = bf16[768,3072]{1,0:T(8,128)(2,1)} async-done(((bf16[24,3072]{1,0:T(8,128)(2,1)}), bf16[768,3072]{1,0:T(8,128)(2,1)}) %all-gather.13.cloned.1.call-update) | async-done | bytes 4718608 | tf_op jit(solution)/shard_map/all_gather | solution.py:98
  246.0 20.9 %multiply_convert_fusion.1 = (bf16[512,3072]{1,0:T(8,128)(2,1)}, f32[512,3072]{1,0:T(8,128)}, f32[512,3072]{1,0:T(8,128)}) fusion(f32[3072]{0:T(1024)S(1)} %convert_element_type.159, bf16[768,3072]{1,0:T(8,128)(2,1)} %all-gather.13.cloned.1.call-done, f32[512,768]{1,0:T(8,128)} %copy-done.7, f32[768]{0:T(1024)S(1)} %convert_element_type.157, ...), kind=kOutput, calls=%fused_computation.14 | convolution fusion | flops 2521694208 | bytes 22042624 | tf_op jit(solution)/shard_map/dot_general | solution.py:32
  266.9 44.4 %all-gather.15.cloned.1.call-done = bf16[3072,768]{1,0:T(8,128)(2,1)} async-done(((bf16[96,768]{1,0:T(8,128)(2,1)}), bf16[3072,768]{1,0:T(8,128)(2,1)}) %all-gather.15.cloned.1.call-update) | async-done | bytes 4718608 | tf_op jit(solution)/shard_map/all_gather | solution.py:100
  311.3 6.1 fusion.43
  321.2 8.5 convert_reduce_fusion
  329.8 3.2 multiply_reduce_fusion.2
  334.7 32.5 %all-gather.17.cloned.1.call-done = bf16[768,768]{1,0:T(8,128)(2,1)} async-done(((bf16[24,768]{1,0:T(8,128)(2,1)}), bf16[768,768]{1,0:T(8,128)(2,1)}) %all-gather.17.cloned.1.call-update) | async-done | bytes 1179664 | tf_op jit(solution)/shard_map/all_gather | solution.py:162
  367.2 3.2 convolution_convert_fusion
  372.7 13.5 %multiply_reduce_fusion = (f32[12,512]{1,0:T(8,128)S(1)}, f32[12,512,512]{1,2,0:T(8,128)}) fusion(f32[12,512]{1,0:T(8,128)S(1)} %log_add_fusion, f32[12,512,512]{1,2,0:T(8,128)} %copy-done, pred[512,512]{0,1:T(8,128)(4,1)S(1)} %broadcast_compare_fusion, bf16[512,12,64]{0,2,1:T(8,128)(2,1)} %bitcast.81, bf16[512,12,64]{0,2,1:T(8,128)(2,1)} %bitcast.80), kind=kOutput, calls=%fused_computation.1 | convolution fusion | flops 418375680 | bytes 27049984 | tf_op jit(solution)/shard_map/qhd,khd->hqk/dot_general | solution.py:186
  386.3 7.0 multiply_convert_fusion
  399.0 3.1 copy.87
  402.4 4.8 multiply_convert_fusion.2
  410.3 3.2 copy.89
  413.6 6.6 convert_reduce_fusion.3
  423.3 3.2 copy.91
  426.5 3.7 fusion.46
  430.3 7.3 fusion.35
  438.7 8.2 fusion.47
  447.1 40.6 %all-reduce.18 = (f32[768]{0:T(1024)S(1)}, f32[768]{0:T(1024)S(1)}, f32[768]{0:T(1024)S(1)}, f32[768]{0:T(1024)S(1)}, f32[768]{0:T(1024)S(1)}, /*index=5*/f32[30...) all-reduce(f32[768]{0:T(1024)S(1)} %reduce_sum.228, ...), channel_id=3, replica_groups=mesh['dp'=4,'fsdp'=8] {'dp','fsdp'}, use_global_device_ids=true, to_apply=%region_15.16.clone | all-reduce | flops 9216 | bytes 73728
  500.8 104.7 %reduce-scatter.21.cloned.1.call-done = f32[24,768]{1,0:T(8,128)} async-done(((f32[768,768]{1,0:T(8,128)}), f32[24,768]{1,0:T(8,128)}) %reduce-scatter.21.cloned.1.call-update) | async-done | bytes 73744
  605.5 103.9 %reduce-scatter.23.cloned.1.call-done = f32[24,768]{1,0:T(8,128)} async-done(((f32[768,768]{1,0:T(8,128)}), f32[24,768]{1,0:T(8,128)}) %reduce-scatter.23.cloned.1.call-update) | async-done | bytes 73744
  709.4 104.7 %reduce-scatter.13.cloned.1.call-done = f32[24,768]{1,0:T(8,128)} async-done(((f32[768,768]{1,0:T(8,128)}), f32[24,768]{1,0:T(8,128)}) %reduce-scatter.13.cloned.1.call-update) | async-done | bytes 73744 | tf_op jit(solution)/shard_map/reduce_scatter | solution.py:225
  814.0 141.0 %reduce-scatter.15.cloned.1.call-done = f32[24,3072]{1,0:T(8,128)} async-done(((f32[768,3072]{1,0:T(8,128)}), f32[24,3072]{1,0:T(8,128)}) %reduce-scatter.15.cloned.1.call-update) | async-done | bytes 294928 | tf_op jit(solution)/shard_map/reduce_scatter | solution.py:229
  955.0 142.1 %reduce-scatter.17.cloned.1.call-done = f32[96,768]{1,0:T(8,128)} async-done(((f32[3072,768]{1,0:T(8,128)}), f32[96,768]{1,0:T(8,128)}) %reduce-scatter.17.cloned.1.call-update) | async-done | bytes 294928 | tf_op jit(solution)/shard_map/reduce_scatter | solution.py:231
  (174 shorter events, 73.9 us)
Async XLA Ops:
  7.2 72.5 %all-gather.7.cloned.1.call-start = ((), (), s32[]{:S(2)}) async-start(), calls=%async_computation.6 | async-start | bytes 1216512 | tf_op jit(solution)/shard_map/all_gather | solution.py:92
  7.9 116.3 %all-gather.9.cloned.1.call-start = ((), (), s32[]{:S(2)}) async-start(), calls=%async_computation.7 | async-start | bytes 1216512 | tf_op jit(solution)/shard_map/all_gather | solution.py:89
  8.7 171.7 %all-gather.11.cloned.1.call-start = ((), (), s32[]{:S(2)}) async-start(), calls=%async_computation.8 | async-start | bytes 1216512 | tf_op jit(solution)/shard_map/all_gather | solution.py:91
  9.4 236.6 %all-gather.13.cloned.1.call-start = ((), (), s32[]{:S(2)}) async-start(), calls=%async_computation.9 | async-start | bytes 4866048 | tf_op jit(solution)/shard_map/all_gather | solution.py:98
  10.0 301.3 %all-gather.15.cloned.1.call-start = ((), (), s32[]{:S(2)}) async-start(), calls=%async_computation.10 | async-start | bytes 4866048 | tf_op jit(solution)/shard_map/all_gather | solution.py:100
  10.6 356.6 %all-gather.17.cloned.1.call-start = ((), (), s32[]{:S(2)}) async-start(), calls=%async_computation.11 | async-start | bytes 1216512 | tf_op jit(solution)/shard_map/all_gather | solution.py:162
  10.6 5.2 collective-permute-start
  16.6 4.5 collective-permute-start.1
  21.2 53.5 %collective-permute-start.2 = (bf16[96,768]{1,0:T(8,128)(2,1)S(1)}, bf16[96,768]{1,0:T(8,128)(2,1)S(1)}, u32[]{:S(2)}, u32[]{:S(2)}) collective-permute-start(bf16[96,768]{1,0:T(8,128)(2,1)S(1)} %maximum_select_fusion.4), channel_id=1, source_target_pairs={{0,4},{1,5},{2,6},{3,7},{4,0},{5,1},{6,2},{7,3},{8,12},{9,13},{10,... | collective-permute-start | bytes 442376 | tf_op jit(solution)/shard_map/ppermute | solution.py:13
  24.3 476.5 %reduce-scatter.19.cloned.1.call-start = ((), (), s32[]{:S(2)}) async-start(), calls=%async_computation.15 | async-start | bytes 2433024
  74.7 1.6 collective-permute-start.3
  77.4 46.9 %copy-start.2 = (bf16[512,768]{1,0:T(8,128)(2,1)S(1)}, bf16[512,768]{1,0:T(8,128)(2,1)}, u32[]{:S(2)}) copy-start(bf16[512,768]{1,0:T(8,128)(2,1)} %param.18) | copy-start | bytes 2359300
  77.4 117.6 %collective-permute-start.4 = (bf16[384,768]{1,0:T(8,128)(2,1)}, bf16[384,768]{1,0:T(8,128)(2,1)}, u32[]{:S(2)}, u32[]{:S(2)}) collective-permute-start(bf16[384,768]{1,0:T(8,128)(2,1)} %maximum_select_fusion.2), channel_id=1, source_target_pairs={{0,16},{1,17},{2,18},{3,19},{4,20},{5,21},{6,22},{7,23},{8,24},{9,... | collective-permute-start | bytes 1769480 | tf_op jit(solution)/shard_map/ppermute | solution.py:13
  82.3 107.1 %copy-start.11 = (bf16[512,768]{0,1:T(8,128)(2,1)}, bf16[512,768]{0,1:T(8,128)(2,1)S(1)}, u32[]{:S(2)}) copy-start(bf16[512,768]{0,1:T(8,128)(2,1)S(1)} %copy.72) | copy-start | bytes 2359300
  186.8 4.6 copy-start
  199.3 112.1 %copy-start.8 = (f32[512,768]{1,0:T(8,128)S(1)}, f32[512,768]{1,0:T(8,128)}, u32[]{:S(2)}) copy-start(f32[512,768]{1,0:T(8,128)} %copy-done.7) | copy-start | bytes 4718596
  311.3 6.4 copy-start.13
  320.3 9.4 slice-start.3
  320.5 9.2 copy-start.19
  321.2 8.5 slice-start.4
  372.7 13.5 %slice-start = ((s8[12582912]{0:T(1024)(128)(4,1)}), s8[4194304]{0:T(1024)(128)(4,1)S(1)}, s32[]{:S(2)}) async-start(s8[12582912]{0:T(1024)(128)(4,1)} %bitcast.71), calls=%async_computation.18 | async-start | bytes 8388608
  372.7 13.5 %slice-start.1 = ((s8[12582912]{0:T(1024)(128)(4,1)}), s8[4194304]{0:T(1024)(128)(4,1)S(1)}, s32[]{:S(2)}) async-start(s8[12582912]{0:T(1024)(128)(4,1)} %bitcast.71), calls=%async_computation.19 | async-start | bytes 8388608
  372.7 13.5 %slice-start.2 = ((s8[12582912]{0:T(1024)(128)(4,1)}), s8[4194304]{0:T(1024)(128)(4,1)S(1)}, s32[]{:S(2)}) async-start(s8[12582912]{0:T(1024)(128)(4,1)} %bitcast.71), calls=%async_computation.20 | async-start | bytes 8388608
  402.1 6.0 copy-start.4
  402.1 203.4 %reduce-scatter.21.cloned.1.call-start = ((), (), s32[]{:S(2)}) async-start(), calls=%async_computation.16 | async-start | bytes 2433024
  413.5 295.9 %reduce-scatter.23.cloned.1.call-start = ((), (), s32[]{:S(2)}) async-start(), calls=%async_computation.17 | async-start | bytes 2433024
  426.5 387.6 %reduce-scatter.13.cloned.1.call-start = ((), (), s32[]{:S(2)}) async-start(), calls=%async_computation.12 | async-start | bytes 2433024 | tf_op jit(solution)/shard_map/reduce_scatter | solution.py:225
  430.3 524.8 %reduce-scatter.15.cloned.1.call-start = ((), (), s32[]{:S(2)}) async-start(), calls=%async_computation.13 | async-start | bytes 9732096 | tf_op jit(solution)/shard_map/reduce_scatter | solution.py:229
  437.6 659.6 %reduce-scatter.17.cloned.1.call-start = ((), (), s32[]{:S(2)}) async-start(), calls=%async_computation.14 | async-start | bytes 9732096 | tf_op jit(solution)/shard_map/reduce_scatter | solution.py:231
  446.9 46.0 %copy-start.17 = (bf16[12,64,512]{2,1,0:T(8,128)(2,1)S(1)}, bf16[12,64,512]{2,1,0:T(8,128)(2,1)}, u32[]{:S(2)}) copy-start(bf16[12,64,512]{2,1,0:T(8,128)(2,1)} %copy-done.16) | copy-start | bytes 2359300
  446.9 48.3 %copy-start.6 = (bf16[12,64,512]{2,1,0:T(8,128)(2,1)S(1)}, bf16[12,64,512]{2,1,0:T(8,128)(2,1)}, u32[]{:S(2)}) copy-start(bf16[12,64,512]{2,1,0:T(8,128)(2,1)} %copy-done.5) | copy-start | bytes 2359300
  487.7 7.5 copy-start.23
  (15 other events, 36.3 us)
Sparse Core Ops, SparseCore 0:
  11.0 57.0 all-gather.6
  71.1 53.1 all-gather.8
  127.3 53.0 all-gather.10
  183.2 62.6 all-gather.12
  248.8 62.4 all-gather.14
  314.2 52.9 all-gather.16
  402.2 98.5 reduce-scatter.18
  507.5 97.9 reduce-scatter.20
  611.4 97.9 reduce-scatter.22
  715.9 98.0 reduce-scatter.12
  820.5 134.4 reduce-scatter.14
  962.4 134.7 reduce-scatter.16
